TPU v7x, 1024 devices: a whole 4x4x32 slice. The times are simulated.
1024 devices in a mesh: fin: 8 (over y, core), fout: 128 (over x, z).
Axes of the slice: x: 4, y: 4, z: 32, core: 2. Of those that a mesh axis runs over, the one named last changes fastest.
Arguments:
- gate_pre: bfloat16 [128, 27648], P('fout', 'fin'), may hold values from -6 to 6
- up_pre: bfloat16 [128, 27648], P('fout', 'fin'), may hold values from -6 to 6
- out_grad: bfloat16 [128, 16384], P(None, 'fout'), may hold values from -12 to 12
- down_weight: bfloat16 [27648, 16384], P('fin', 'fout'), may hold values from -0.0390625 to 0.0390625
Outputs:
- gate_grad: bfloat16 [128, 27648], P('fout', 'fin')
- up_grad: bfloat16 [128, 27648], P('fout', 'fin')
- down_grad: bfloat16 [27648, 16384], P('fin', 'fout')
All inputs are finite; a program needn't handle non-finite values.
Results may differ from a plain program's by a relative error of at most 0.0049.
Values may be sent and summed in bfloat16 or wider, within the bound.
A program may use at most 32 MiB of HBM per device.

v0:
```python
import jax
import jax.numpy as jnp
from jax import lax
from jax.sharding import PartitionSpec as P


def swiglu_back(gate_pre, up_pre, upstream):
    gate_float = gate_pre.astype(jnp.float32)
    up_float = up_pre.astype(jnp.float32)
    logistic = jax.nn.sigmoid(gate_float)
    activated = gate_float * logistic
    gate_grad = (upstream * up_float * logistic * (1.0 + gate_float * (1.0 - logistic))).astype(
        jnp.bfloat16
    )
    up_grad = (upstream * activated).astype(jnp.bfloat16)
    hidden = (activated * up_float).astype(jnp.bfloat16)
    return (gate_grad, up_grad, hidden)


def grad_times(grad_rows, hidden_rows):
    return lax.dot_general(
        grad_rows, hidden_rows, (((0,), (0,)), ((), ())), preferred_element_type=jnp.float32
    )


def local(gate_pre, up_pre, out_grad, down_weight):
    grad_rows = out_grad
    upstream = lax.psum_scatter(
        lax.dot_general(
            grad_rows, down_weight, (((1,), (1,)), ((), ())), preferred_element_type=jnp.float32
        ),
        "fout",
        scatter_dimension=0,
        tiled=True,
    )
    gate_grad, up_grad, hidden = swiglu_back(gate_pre, up_pre, upstream)
    grad_rows = out_grad
    weight_trans = grad_times(grad_rows, lax.all_gather(hidden, "fout", axis=0, tiled=True))
    down_grad = weight_trans.T.astype(jnp.bfloat16)
    return (gate_grad, up_grad, down_grad)


def solution(mesh):
    placed = (P("fout", "fin"), P("fout", "fin"), P(None, "fout"), P("fin", "fout"))
    return jax.shard_map(
        local,
        mesh=mesh,
        in_specs=placed,
        out_specs=(P("fout", "fin"), P("fout", "fin"), P("fin", "fout")),
        check_vma=False,
    )
```

profile of v0, /device:TPU:16, one launch (start us, length us, event | category | flops | bytes accessed | tf_op | source)
XLA Modules:
  0.0 541.0 jit_solution(7074751343718147602)
XLA Ops:
  7.2 0.0 copy-start
  7.2 0.0 copy-start.2
  7.2 0.0 copy-start.3
  7.2 0.0 all-reduce.3.cloned.1.call-start
  7.2 1.1 copy-done
  8.3 2.4 fusion.2
  10.7 0.0 copy-start.1
  10.7 0.0 all-reduce.3.cloned.1.call-update
  10.7 1.4 dynamic-slice
  12.1 0.0 copy-done.2
  12.1 0.0 copy-done.3
  12.1 216.3 %all-gather = bf16[128,1,3456]{2,1,0:T(2,128)(2,1)S(1)} all-gather(bf16[1,1,3456]{2,1,0:T(2,128)(2,1)S(1)} %get-tuple-element.3), channel_id=1, replica_groups=mesh['fin'=8,'fout'=128] {'fout'}, dimensions={0}, use_global_device_ids=true | all-gather | bytes 891648 | tf_op jit(solution)/shard_map/all_gather | solution.py:38
  228.4 0.0 copy-done.1
  228.4 1.3 convolution_convert_fusion
  229.8 302.2 %all-reduce.3.cloned.1.call-done = f32[128,3456]{1,0:T(8,128)} async-done(((f32[128,3456]{1,0:T(8,128)}), f32[128,3456]{1,0:T(8,128)}) %all-reduce.3.cloned.1.call-update) | async-done | bytes 1769488
  531.9 2.2 multiply_convert_fusion
  (1 shorter events, 0.0 us)
Async XLA Ops:
  7.2 1.2 copy-start
  7.2 4.9 copy-start.2
  7.2 4.9 copy-start.3
  7.2 524.7 %all-reduce.3.cloned.1.call-start = ((), (), s32[]{:S(2)}) async-start(), calls=%async_computation | async-start | bytes 3538944
  10.7 217.7 %copy-start.1 = (bf16[128,128]{1,0:T(8,128)(2,1)S(1)}, bf16[128,128]{1,0:T(8,128)(2,1)}, u32[]{:S(2)}) copy-start(bf16[128,128]{1,0:T(8,128)(2,1)} %param.6) | copy-start | bytes 98308
Sparse Core Ops, SparseCore 0:
  11.4 520.4 all-reduce.2
where the time goes:
time: 541 us
  waiting for transfers between devices  302 us (56%)
  blocking collectives  216 us (40%)
  between operations  14.1 us (3%)
    unnamed x2, waiting for transfers between devices  302 us
    all_gather x1, blocking collectives, local(): lax.all_gather(hidden, 'fout', axis=0, tiled=True)  216 us
  transfers between devices with their start and end apart: 1, of which 1 were waited for; matrix products, arithmetic and copies ran while one was open for 1% of the time, Pallas kernels for 0%

commit v1 on v0

v1 whole, which is shorter than its diff:
```python
import jax
import jax.numpy as jnp
from jax import lax
from jax.experimental import pallas as pl
from jax.experimental.pallas import tpu as pltpu
from jax.sharding import PartitionSpec as P

MESH = pl.DeviceIdType.MESH
F32, BF16 = jnp.float32, jnp.bfloat16
NX, NZ = 4, 32
TOK = 128
UNITS = 3456
LANES = 128
CHUNKS = UNITS // LANES
ROWS = 32
HALF = 16


def slot(b, h, k, j=0):
    return (((b * 2 + h) * 4 + k) * 4 + j) * ROWS


def kernel(
    g_ref, u_ref, og_ref, w_ref, gg_ref, ug_ref, dg_ref,
    ogp, part, psend, xrecv, spread, zsend, brecv, asend, arecv, gs, us, outs, held, held32,
    x_send, x_recv, b_send, b_recv, a_send, a_recv,
    ga_send, ga_recv, gb_send, gb_recv, gx_send, gx_recv,
):
    f = lax.axis_index("fout")
    x, z = f // NZ, lax.rem(f, NZ)
    group, cls = z // 4, lax.rem(z, 4)

    def at(dx, dz):
        return {"fout": lax.rem(x + dx + NX, NX) * NZ + lax.rem(z + dz + NZ, NZ)}

    def copy(src, dst, send, recv, device):
        return pltpu.make_async_remote_copy(
            src_ref=src, dst_ref=dst, send_sem=send, recv_sem=recv,
            device_id=device, device_id_type=MESH,
        )

    barrier = pltpu.get_barrier_semaphore()
    peers = [(d, 0) for d in (1, 2, 3)] + [(0, d) for d in (1, -1, 2, -2, 4, -4, 8, -8, 12, -12, 16)]
    for dx, dz in peers:
        pl.semaphore_signal(barrier, inc=1, device_id=at(dx, dz), device_id_type=MESH)

    gs[...] = jnp.zeros_like(gs)
    us[...] = jnp.zeros_like(us)
    for c in range(CHUNKS):
        cols = slice(c * LANES, (c + 1) * LANES)
        gs[c : c + 1, :] = g_ref[:, cols].astype(F32)
        us[c : c + 1, :] = u_ref[:, cols].astype(F32)
    gate, up = gs[...], us[...]
    logistic = 1.0 / (1.0 + jnp.exp(-gate))
    activated = gate * logistic
    mine = pl.multiple_of(group * ROWS + (group // 4) * (12 * ROWS), ROWS)
    held[pl.ds(mine, ROWS), :] = (activated * up).astype(BF16)

    row = lax.broadcasted_iota(jnp.int32, (TOK, TOK), 0)
    token = (
        32 * lax.rem(row // 32 + x, NX)
        + 16 * lax.rem(row // 16, 2)
        + lax.rem(lax.rem(row // 4, 4) + cls, 4)
        + 4 * lax.rem(row, 4)
    )
    pick = (lax.broadcasted_iota(jnp.int32, (TOK, TOK), 1) == token).astype(F32).astype(BF16)
    ogp[...] = jnp.dot(pick, og_ref[...], preferred_element_type=F32).astype(BF16)

    for c in range(CHUNKS):
        cols = slice(c * LANES, (c + 1) * LANES)
        product = lax.dot_general(
            ogp[...], w_ref[cols, :], (((1,), (1,)), ((), ())), preferred_element_type=F32
        )
        part[:, cols] = product[0:32, :]
        psend[:, cols] = product[32:, :].astype(BF16)

    pl.semaphore_wait(barrier, len(peers))

    def x_copy(d, h):
        rows = pl.ds((d - 1) * 32 + h * HALF, HALF)
        return copy(psend.at[rows], xrecv.at[rows], x_send.at[d - 1, h], x_recv.at[d - 1, h], at(d, 0))

    def b_copy(h, k):
        dz = {1: 1, 3: -1, 2: 2 if h == 0 else -2}[k]
        rows = pl.ds(slot(0, h, k), 4 * ROWS)
        return copy(zsend.at[rows], brecv.at[rows], b_send.at[h, k], b_recv.at[h, k], at(0, dz))

    def a_copy(h, j):
        src = asend.at[pl.ds((h * 4 + j) * ROWS, ROWS)]
        dst = arecv.at[pl.ds(pl.multiple_of(group * ROWS, ROWS), ROWS)]
        target = {"fout": x * NZ + 16 * h + 4 * j + cls}
        return copy(src, dst, a_send.at[h * 4 + j], a_recv.at[group], target)

    def ga_copy(j):
        rows = pl.ds(mine, ROWS)
        target = {"fout": x * NZ + 4 * j + cls}
        return copy(held.at[rows], held.at[rows], ga_send.at[j], ga_recv.at[group], target)

    def ga_wait(j):
        rows = pl.ds(slot(0, j // 4, 0, j % 4), ROWS)
        return copy(held.at[rows], held.at[rows], ga_send.at[j], ga_recv.at[j], at(0, 1))

    def gb_copy(h, k):
        dz = {1: -1, 3: 1, 2: 2 if h == 0 else -2}[k]
        src, dst = pl.ds(slot(0, h, 0), 4 * ROWS), pl.ds(slot(0, h, k), 4 * ROWS)
        return copy(held.at[src], held.at[dst], gb_send.at[h, k], gb_recv.at[h, k], at(0, dz))

    def gx_copy(b, h, k):
        src, dst = pl.ds(slot(0, h, k), 4 * ROWS), pl.ds(slot(b, h, k), 4 * ROWS)
        return copy(held.at[src], held.at[dst], gx_send.at[b, h, k], gx_recv.at[b, h, k], at(-b, 0))

    def unpack(b, h, k):
        rows = pl.ds(slot(b, h, k), 4 * ROWS)
        held32[rows, :] = held[rows, :].astype(F32)

    def start_x():
        for h in (0, 1):
            for d in (2, 1, 3):
                x_copy(d, h).start()

    def start_gather():
        for j in range(8):
            @pl.when(group != j)
            def _():
                ga_copy(j).start()

    def sum_x(h):
        for d in (1, 3, 2):
            x_copy(d, h).wait_recv()
        for c in range(CHUNKS):
            cols = slice(c * LANES, (c + 1) * LANES)
            total = part[h * HALF : (h + 1) * HALF, cols]
            for d in (1, 2, 3):
                start = (d - 1) * 32 + h * HALF
                total += xrecv[start : start + HALF, cols].astype(F32)
            spread[pl.ds(h * HALF * ROWS + c, HALF, stride=ROWS), :] = total
        first = slot(0, h, 1)
        rows = pl.ds(first, 12 * ROWS)
        zsend[rows, :] = spread[rows, :].astype(BF16)
        for k in (2, 1, 3):
            b_copy(h, k).start()

    def sum_b(h):
        for k in (1, 3, 2):
            b_copy(h, k).wait_recv()
        total = spread[pl.ds(slot(0, h, 0), 4 * ROWS), :]
        for k in (1, 2, 3):
            total += brecv[pl.ds(slot(0, h, k), 4 * ROWS), :].astype(F32)
        asend[pl.ds(h * 4 * ROWS, 4 * ROWS), :] = total.astype(BF16)
        for j in range(4):
            @pl.when(group != h * 4 + j)
            def _():
                a_copy(h, j).start()

            @pl.when(group == h * 4 + j)
            def _():
                arecv[pl.ds((h * 4 + j) * ROWS, ROWS), :] = asend[pl.ds((h * 4 + j) * ROWS, ROWS), :]

    def gather_a(h):
        for j in range(4 * h, 4 * h + 4):
            @pl.when(group != j)
            def _():
                ga_wait(j).wait_recv()
        for k in (2, 1, 3):
            gb_copy(h, k).start()
        for b in (2, 1, 3):
            gx_copy(b, h, 0).start()
        unpack(0, h, 0)

    def gather_b(h, k):
        gb_copy(h, k).wait_recv()
        for b in (2, 1, 3):
            gx_copy(b, h, k).start()
        unpack(0, h, k)

    def finish_sums():
        for j in range(8):
            @pl.when(group != j)
            def _():
                rows = pl.ds(j * ROWS, ROWS)
                copy(asend.at[rows], arecv.at[rows], a_send.at[j], a_recv.at[j], at(0, 1)).wait_recv()
        upstream = arecv[0:ROWS, :].astype(F32)
        for j in range(1, 8):
            upstream += arecv[j * ROWS : (j + 1) * ROWS, :].astype(F32)
        gate, up = gs[...], us[...]
        logistic = 1.0 / (1.0 + jnp.exp(-gate))
        outs[0:ROWS, :] = upstream * up * logistic * (1.0 + gate * (1.0 - logistic))
        outs[ROWS:, :] = upstream * (gate * logistic)
        for c in range(CHUNKS):
            cols = slice(c * LANES, (c + 1) * LANES)
            gg_ref[:, cols] = outs[c : c + 1, :].astype(BF16)
            ug_ref[:, cols] = outs[ROWS + c : ROWS + c + 1, :].astype(BF16)

    start_gather()
    start_x()
    sum_x(0)
    sum_x(1)
    sum_b(0)
    sum_b(1)
    gather_a(0)
    gather_a(1)
    for h in (0, 1):
        for k in (1, 3, 2):
            gather_b(h, k)
    finish_sums()
    for b in (1, 3, 2):
        for h in (0, 1):
            for k in range(4):
                gx_copy(b, h, k).wait_recv()
                unpack(b, h, k)

    for c in range(CHUNKS):
        hidden = held32[pl.ds(c, TOK, stride=ROWS), :].astype(BF16)
        grad = lax.dot_general(
            hidden, ogp[...], (((0,), (0,)), ((), ())), preferred_element_type=F32
        )
        dg_ref[c * LANES : (c + 1) * LANES, :] = grad.astype(BF16)

    for h in (0, 1):
        for d in (1, 2, 3):
            x_copy(d, h).wait_send()
        for k in (1, 2, 3):
            b_copy(h, k).wait_send()
            gb_copy(h, k).wait_send()
        for j in range(4):
            @pl.when(group != h * 4 + j)
            def _():
                a_copy(h, j).wait_send()
                ga_copy(h * 4 + j).wait_send()
        for b in (1, 2, 3):
            for k in range(4):
                gx_copy(b, h, k).wait_send()


def local(gate_pre, up_pre, out_grad, down_weight):
    dma = pltpu.SemaphoreType.DMA
    vmem = pl.BlockSpec(memory_space=pltpu.VMEM)
    return pl.pallas_call(
        kernel,
        out_shape=(
            jax.ShapeDtypeStruct((1, UNITS), BF16),
            jax.ShapeDtypeStruct((1, UNITS), BF16),
            jax.ShapeDtypeStruct((UNITS, LANES), BF16),
        ),
        in_specs=[vmem] * 4,
        out_specs=(vmem,) * 3,
        scratch_shapes=[
            pltpu.VMEM((TOK, LANES), BF16),
            pltpu.VMEM((32, UNITS), F32),
            pltpu.VMEM((96, UNITS), BF16),
            pltpu.VMEM((96, UNITS), BF16),
            pltpu.VMEM((32 * ROWS, LANES), F32),
            pltpu.VMEM((32 * ROWS, LANES), BF16),
            pltpu.VMEM((32 * ROWS, LANES), BF16),
            pltpu.VMEM((8 * ROWS, LANES), BF16),
            pltpu.VMEM((8 * ROWS, LANES), BF16),
            pltpu.VMEM((ROWS, LANES), F32),
            pltpu.VMEM((ROWS, LANES), F32),
            pltpu.VMEM((2 * ROWS, LANES), F32),
            pltpu.VMEM((TOK * ROWS, LANES), BF16),
            pltpu.VMEM((TOK * ROWS, LANES), F32),
            dma((3, 2)), dma((3, 2)),
            dma((2, 4)), dma((2, 4)),
            dma((8,)), dma((8,)),
            dma((8,)), dma((8,)),
            dma((2, 4)), dma((2, 4)),
            dma((4, 2, 4)), dma((4, 2, 4)),
        ],
        compiler_params=pltpu.CompilerParams(
            collective_id=0, has_side_effects=True, vmem_limit_bytes=40 * 2**20
        ),
    )(gate_pre, up_pre, out_grad, down_weight)


def solution(mesh):
    placed = (P("fout", "fin"), P("fout", "fin"), P(None, "fout"), P("fin", "fout"))
    return jax.shard_map(
        local,
        mesh=mesh,
        in_specs=placed,
        out_specs=(P("fout", "fin"), P("fout", "fin"), P("fin", "fout")),
        check_vma=False,
    )
```

time: 541 us -> 70.2 us (0.13)
  the two profiles are of different devices: /device:TPU:16 before, /device:TPU:26 now
where the time goes in v1:
time: 70.2 us; the launch traced here: 69.8 us
  Pallas kernels  63.7 us (91%)
  local copies, waits for them, and re-layouts  5.45 us (8%)
    pallas_call x1, Pallas kernels, local(): pl.pallas_call(kernel, out_shape=(jax.ShapeDtypeStruct((1, UNITS), BF16),...  63.7 us
    unnamed x11, local copies, waits for them, and re-layouts  5.45 us

profile of v1, /device:TPU:26, one launch (start us, length us, event | category | flops | bytes accessed | tf_op | source)
XLA Modules:
  0.0 69.8 jit_solution(606617313764946382)
XLA Ops:
  0.6 0.0 copy-start
  0.6 1.2 %copy-done = bf16[3456,128]{1,0:T(8,128)(2,1)S(1)} copy-done((bf16[3456,128]{1,0:T(8,128)(2,1)S(1)}, bf16[3456,128]{1,0:T(8,128)(2,1)}, u32[]{:S(2)}) %copy-start) | copy-done | bytes 884760
  1.8 0.0 copy-start.1
  1.8 0.8 %copy-done.1 = bf16[128,128]{1,0:T(8,128)(2,1)S(1)} copy-done((bf16[128,128]{1,0:T(8,128)(2,1)S(1)}, bf16[128,128]{1,0:T(8,128)(2,1)}, u32[]{:S(2)}) %copy-start.1) | copy-done | bytes 32792
  2.6 0.0 copy-start.2
  2.6 0.7 %copy-done.2 = bf16[1,3456]{1,0:T(2,128)(2,1)S(1)} copy-done((bf16[1,3456]{1,0:T(2,128)(2,1)S(1)}, bf16[1,3456]{1,0:T(2,128)(2,1)}, u32[]{:S(2)}) %copy-start.2) | copy-done | bytes 6936
  3.3 0.0 copy-start.3
  3.3 0.7 %copy-done.3 = bf16[1,3456]{1,0:T(2,128)(2,1)S(1)} copy-done((bf16[1,3456]{1,0:T(2,128)(2,1)S(1)}, bf16[1,3456]{1,0:T(2,128)(2,1)}, u32[]{:S(2)}) %copy-start.3) | copy-done | bytes 6936
  4.0 63.7 %shard_map.67 = (bf16[1,3456]{1,0:T(2,128)(2,1)S(1)}, bf16[1,3456]{1,0:T(2,128)(2,1)S(1)}, bf16[3456,128]{1,0:T(8,128)(2,1)S(1)}) custom-call(bf16[1,3456]{1,0:T(2,128)(2,1)S(1)} %copy-done.2, bf16[1,3456]{1,0:T(2,128)(2,1)S(1)} %copy-done.3, bf16[128,128]{1,0:T(8,128)(2,1)S(1)} %copy-done.1, bf16[3456,128]{1,0:T(8,128)(2,1)S(1)} %copy-done), custom_call_target="tpu_custom_call" | custom-call | tf_op jit(solution)/shard_map/pallas_call | solution.py:238
  67.7 0.6 copy.10
  68.3 0.6 copy.11
  68.9 0.9 %copy.12 = bf16[3456,128]{1,0:T(8,128)(2,1)} copy(bf16[3456,128]{1,0:T(8,128)(2,1)S(1)} %get-tuple-element.8) | data formatting | bytes 1769472
Async XLA Ops:
  0.6 1.2 %copy-start = (bf16[3456,128]{1,0:T(8,128)(2,1)S(1)}, bf16[3456,128]{1,0:T(8,128)(2,1)}, u32[]{:S(2)}) copy-start(bf16[3456,128]{1,0:T(8,128)(2,1)} %w_ref.1) | copy-start | bytes 2654212
  1.8 0.8 %copy-start.1 = (bf16[128,128]{1,0:T(8,128)(2,1)S(1)}, bf16[128,128]{1,0:T(8,128)(2,1)}, u32[]{:S(2)}) copy-start(bf16[128,128]{1,0:T(8,128)(2,1)} %og_ref.1) | copy-start | bytes 98308
  2.6 0.7 %copy-start.2 = (bf16[1,3456]{1,0:T(2,128)(2,1)S(1)}, bf16[1,3456]{1,0:T(2,128)(2,1)}, u32[]{:S(2)}) copy-start(bf16[1,3456]{1,0:T(2,128)(2,1)} %g_ref.1) | copy-start | bytes 20740
  3.3 0.7 %copy-start.3 = (bf16[1,3456]{1,0:T(2,128)(2,1)S(1)}, bf16[1,3456]{1,0:T(2,128)(2,1)}, u32[]{:S(2)}) copy-start(bf16[1,3456]{1,0:T(2,128)(2,1)} %u_ref.1) | copy-start | bytes 20740

commit v2 on v1

--- a/solution.py
+++ b/solution.py
@@ -14,6 +14,7 @@
 CHUNKS = UNITS // LANES
 ROWS = 32
 HALF = 16
+GROUPS = NZ // 4
 
 
 def slot(b, h, k, j=0):
@@ -21,9 +22,10 @@
 
 
 def kernel(
-    g_ref, u_ref, og_ref, w_ref, gg_ref, ug_ref, dg_ref,
+    g_hbm, u_hbm, og_hbm, w_hbm, gg_ref, ug_ref, dg_ref,
+    g_ref, u_ref, og_ref, w_ref,
     ogp, part, psend, xrecv, spread, zsend, brecv, asend, arecv, gs, us, outs, held, held32,
-    x_send, x_recv, b_send, b_recv, a_send, a_recv,
+    in_sem, x_send, x_recv, b_send, b_recv, a_send, a_recv,
     ga_send, ga_recv, gb_send, gb_recv, gx_send, gx_recv,
 ):
     f = lax.axis_index("fout")
@@ -39,13 +41,42 @@
             device_id=device, device_id_type=MESH,
         )
 
+    def signal(sem, device):
+        pl.semaphore_signal(sem, inc=1, device_id=device, device_id_type=MESH)
+
+    def beside(k):
+        return at(0, lax.rem(cls + k, 4) - cls)
+
     barrier = pltpu.get_barrier_semaphore()
-    peers = [(d, 0) for d in (1, 2, 3)] + [(0, d) for d in (1, -1, 2, -2, 4, -4, 8, -8, 12, -12, 16)]
-    for dx, dz in peers:
-        pl.semaphore_signal(barrier, inc=1, device_id=at(dx, dz), device_id_type=MESH)
+    for d in (1, 2, 3):
+        signal(barrier, beside(d))
+    for d in (1, 2, 3):
+        signal(barrier, at(d, 0))
+    for m in range(1, GROUPS):
+        @pl.when(group + m < GROUPS)
+        def _():
+            signal(barrier, at(0, 4 * m))
+
+    fetch = [
+        pltpu.make_async_copy(src, dst, in_sem.at[i])
+        for i, (src, dst) in enumerate(((w_hbm, w_ref), (og_hbm, og_ref), (g_hbm, g_ref), (u_hbm, u_ref)))
+    ]
+    for c in fetch:
+        c.start()
+
+    row = lax.broadcasted_iota(jnp.int32, (TOK, TOK), 0)
+    token = (
+        32 * lax.rem(row // 32 + x, NX)
+        + 16 * lax.rem(row // 16, 2)
+        + lax.rem(lax.rem(row // 4, 4) + cls, 4)
+        + 4 * lax.rem(row, 4)
+    )
+    pick = (lax.broadcasted_iota(jnp.int32, (TOK, TOK), 1) == token).astype(F32).astype(BF16)
 
     gs[...] = jnp.zeros_like(gs)
     us[...] = jnp.zeros_like(us)
+    fetch[2].wait()
+    fetch[3].wait()
     for c in range(CHUNKS):
         cols = slice(c * LANES, (c + 1) * LANES)
         gs[c : c + 1, :] = g_ref[:, cols].astype(F32)
@@ -56,16 +87,10 @@
     mine = pl.multiple_of(group * ROWS + (group // 4) * (12 * ROWS), ROWS)
     held[pl.ds(mine, ROWS), :] = (activated * up).astype(BF16)
 
-    row = lax.broadcasted_iota(jnp.int32, (TOK, TOK), 0)
-    token = (
-        32 * lax.rem(row // 32 + x, NX)
-        + 16 * lax.rem(row // 16, 2)
-        + lax.rem(lax.rem(row // 4, 4) + cls, 4)
-        + 4 * lax.rem(row, 4)
-    )
-    pick = (lax.broadcasted_iota(jnp.int32, (TOK, TOK), 1) == token).astype(F32).astype(BF16)
+    fetch[1].wait()
     ogp[...] = jnp.dot(pick, og_ref[...], preferred_element_type=F32).astype(BF16)
 
+    fetch[0].wait()
     for c in range(CHUNKS):
         cols = slice(c * LANES, (c + 1) * LANES)
         product = lax.dot_general(
@@ -74,16 +99,15 @@
         part[:, cols] = product[0:32, :]
         psend[:, cols] = product[32:, :].astype(BF16)
 
-    pl.semaphore_wait(barrier, len(peers))
+    pl.semaphore_wait(barrier, 6 + group)
 
     def x_copy(d, h):
         rows = pl.ds((d - 1) * 32 + h * HALF, HALF)
         return copy(psend.at[rows], xrecv.at[rows], x_send.at[d - 1, h], x_recv.at[d - 1, h], at(d, 0))
 
     def b_copy(h, k):
-        dz = {1: 1, 3: -1, 2: 2 if h == 0 else -2}[k]
         rows = pl.ds(slot(0, h, k), 4 * ROWS)
-        return copy(zsend.at[rows], brecv.at[rows], b_send.at[h, k], b_recv.at[h, k], at(0, dz))
+        return copy(zsend.at[rows], brecv.at[rows], b_send.at[h, k], b_recv.at[h, k], beside(k))
 
     def a_copy(h, j):
         src = asend.at[pl.ds((h * 4 + j) * ROWS, ROWS)]
@@ -101,9 +125,8 @@
         return copy(held.at[rows], held.at[rows], ga_send.at[j], ga_recv.at[j], at(0, 1))
 
     def gb_copy(h, k):
-        dz = {1: -1, 3: 1, 2: 2 if h == 0 else -2}[k]
         src, dst = pl.ds(slot(0, h, 0), 4 * ROWS), pl.ds(slot(0, h, k), 4 * ROWS)
-        return copy(held.at[src], held.at[dst], gb_send.at[h, k], gb_recv.at[h, k], at(0, dz))
+        return copy(held.at[src], held.at[dst], gb_send.at[h, k], gb_recv.at[h, k], beside(4 - k))
 
     def gx_copy(b, h, k):
         src, dst = pl.ds(slot(0, h, k), 4 * ROWS), pl.ds(slot(b, h, k), 4 * ROWS)
@@ -112,17 +135,6 @@
     def unpack(b, h, k):
         rows = pl.ds(slot(b, h, k), 4 * ROWS)
         held32[rows, :] = held[rows, :].astype(F32)
-
-    def start_x():
-        for h in (0, 1):
-            for d in (2, 1, 3):
-                x_copy(d, h).start()
-
-    def start_gather():
-        for j in range(8):
-            @pl.when(group != j)
-            def _():
-                ga_copy(j).start()
 
     def sum_x(h):
         for d in (1, 3, 2):
@@ -134,8 +146,7 @@
                 start = (d - 1) * 32 + h * HALF
                 total += xrecv[start : start + HALF, cols].astype(F32)
             spread[pl.ds(h * HALF * ROWS + c, HALF, stride=ROWS), :] = total
-        first = slot(0, h, 1)
-        rows = pl.ds(first, 12 * ROWS)
+        rows = pl.ds(slot(0, h, 1), 12 * ROWS)
         zsend[rows, :] = spread[rows, :].astype(BF16)
         for k in (2, 1, 3):
             b_copy(h, k).start()
@@ -148,7 +159,7 @@
             total += brecv[pl.ds(slot(0, h, k), 4 * ROWS), :].astype(F32)
         asend[pl.ds(h * 4 * ROWS, 4 * ROWS), :] = total.astype(BF16)
         for j in range(4):
-            @pl.when(group != h * 4 + j)
+            @pl.when(group > h * 4 + j)
             def _():
                 a_copy(h, j).start()
 
@@ -156,22 +167,33 @@
             def _():
                 arecv[pl.ds((h * 4 + j) * ROWS, ROWS), :] = asend[pl.ds((h * 4 + j) * ROWS, ROWS), :]
 
+    def above(h):
+        for j in range(4 * h, 4 * h + 4):
+            @pl.when(group < j)
+            def _():
+                ga_wait(j).wait_recv()
+                ga_copy(j).start()
+                a_copy(h, j - 4 * h).start()
+
+    def below(h):
+        for j in range(4 * h, 4 * h + 4):
+            @pl.when(group > j)
+            def _():
+                ga_wait(j).wait_recv()
+
     def gather_a(h):
-        for j in range(4 * h, 4 * h + 4):
-            @pl.when(group != j)
-            def _():
-                ga_wait(j).wait_recv()
         for k in (2, 1, 3):
             gb_copy(h, k).start()
         for b in (2, 1, 3):
             gx_copy(b, h, 0).start()
         unpack(0, h, 0)
 
-    def gather_b(h, k):
-        gb_copy(h, k).wait_recv()
-        for b in (2, 1, 3):
-            gx_copy(b, h, k).start()
-        unpack(0, h, k)
+    def gather_b(h):
+        for k in (1, 3, 2):
+            gb_copy(h, k).wait_recv()
+            for b in (2, 1, 3):
+                gx_copy(b, h, k).start()
+            unpack(0, h, k)
 
     def finish_sums():
         for j in range(8):
@@ -191,17 +213,40 @@
             gg_ref[:, cols] = outs[c : c + 1, :].astype(BF16)
             ug_ref[:, cols] = outs[ROWS + c : ROWS + c + 1, :].astype(BF16)
 
-    start_gather()
-    start_x()
-    sum_x(0)
-    sum_x(1)
-    sum_b(0)
-    sum_b(1)
-    gather_a(0)
-    gather_a(1)
+    for j in range(GROUPS - 1):
+        @pl.when(group > j)
+        def _():
+            ga_copy(j).start()
+    for d in (2, 1, 3):
+        x_copy(d, 0).start()
+    for d in (2, 1, 3):
+        x_copy(d, 0).wait_send()
+    for d in (2, 1, 3):
+        x_copy(d, 1).start()
     for h in (0, 1):
-        for k in (1, 3, 2):
-            gather_b(h, k)
+        sum_x(h)
+        sum_b(h)
+
+    @pl.when(group < 3)
+    def _():
+        above(0)
+        below(0)
+        gather_a(0)
+        gather_b(0)
+        above(1)
+        gather_a(1)
+        gather_b(1)
+
+    @pl.when(group >= 3)
+    def _():
+        above(1)
+        below(1)
+        gather_a(1)
+        gather_b(1)
+        below(0)
+        gather_a(0)
+        gather_b(0)
+
     finish_sums()
     for b in (1, 3, 2):
         for h in (0, 1):
@@ -217,8 +262,9 @@
         dg_ref[c * LANES : (c + 1) * LANES, :] = grad.astype(BF16)
 
     for h in (0, 1):
-        for d in (1, 2, 3):
-            x_copy(d, h).wait_send()
+        if h == 1:
+            for d in (1, 2, 3):
+                x_copy(d, h).wait_send()
         for k in (1, 2, 3):
             b_copy(h, k).wait_send()
             gb_copy(h, k).wait_send()
@@ -226,25 +272,38 @@
             @pl.when(group != h * 4 + j)
             def _():
                 a_copy(h, j).wait_send()
-                ga_copy(h * 4 + j).wait_send()
         for b in (1, 2, 3):
             for k in range(4):
                 gx_copy(b, h, k).wait_send()
+    for j in range(GROUPS):
+        @pl.when(group != j)
+        def _():
+            ga_copy(j).wait_send()
 
 
 def local(gate_pre, up_pre, out_grad, down_weight):
     dma = pltpu.SemaphoreType.DMA
     vmem = pl.BlockSpec(memory_space=pltpu.VMEM)
+    shapes = (
+        jax.ShapeDtypeStruct((1, UNITS), BF16),
+        jax.ShapeDtypeStruct((1, UNITS), BF16),
+        jax.ShapeDtypeStruct((UNITS, LANES), BF16),
+    )
+    anywhere = pl.BlockSpec(memory_space=pl.ANY)
+    operands = [
+        pltpu.with_memory_space_constraint(a, pltpu.HBM)
+        for a in (gate_pre, up_pre, out_grad, down_weight)
+    ]
     return pl.pallas_call(
         kernel,
-        out_shape=(
-            jax.ShapeDtypeStruct((1, UNITS), BF16),
-            jax.ShapeDtypeStruct((1, UNITS), BF16),
-            jax.ShapeDtypeStruct((UNITS, LANES), BF16),
-        ),
-        in_specs=[vmem] * 4,
+        out_shape=shapes,
+        in_specs=[anywhere] * 4,
         out_specs=(vmem,) * 3,
         scratch_shapes=[
+            pltpu.VMEM((1, UNITS), BF16),
+            pltpu.VMEM((1, UNITS), BF16),
+            pltpu.VMEM((TOK, LANES), BF16),
+            pltpu.VMEM((UNITS, LANES), BF16),
             pltpu.VMEM((TOK, LANES), BF16),
             pltpu.VMEM((32, UNITS), F32),
             pltpu.VMEM((96, UNITS), BF16),
@@ -259,6 +318,7 @@
             pltpu.VMEM((2 * ROWS, LANES), F32),
             pltpu.VMEM((TOK * ROWS, LANES), BF16),
             pltpu.VMEM((TOK * ROWS, LANES), F32),
+            dma((4,)),
             dma((3, 2)), dma((3, 2)),
             dma((2, 4)), dma((2, 4)),
             dma((8,)), dma((8,)),
@@ -267,9 +327,9 @@
             dma((4, 2, 4)), dma((4, 2, 4)),
         ],
         compiler_params=pltpu.CompilerParams(
-            collective_id=0, has_side_effects=True, vmem_limit_bytes=40 * 2**20
+            collective_id=0, has_side_effects=True, vmem_limit_bytes=32 * 2**20
         ),
-    )(gate_pre, up_pre, out_grad, down_weight)
+    )(*operands)
 
 
 def solution(mesh):

time: 70.2 us -> 61.3 us (0.87)
  the two profiles are of different devices: /device:TPU:26 before, /device:TPU:992 now
where the time goes in v2:
time: 61.3 us; the launch traced here: 61.1 us
  Pallas kernels  58.4 us (95%)
  local copies, waits for them, and re-layouts  2.11 us (3%)
  between operations  0.64 us (1%)
    pallas_call x1, Pallas kernels, local(): pl.pallas_call(kernel, out_shape=shapes, in_specs=[anywhere] * 4, out_spe...  58.4 us
    unnamed x3, local copies, waits for them, and re-layouts  2.11 us

profile of v2, /device:TPU:992, one launch (start us, length us, event | category | flops | bytes accessed | tf_op | source)
XLA Modules:
  0.0 61.1 jit_solution(8062617119647439073)
XLA Ops:
  0.6 58.4 %shard_map.67 = (bf16[1,3456]{1,0:T(2,128)(2,1)S(1)}, bf16[1,3456]{1,0:T(2,128)(2,1)S(1)}, bf16[3456,128]{1,0:T(8,128)(2,1)S(1)}) custom-call(bf16[1,3456]{1,0:T(2,128)(2,1)} %g_hbm.1, bf16[1,3456]{1,0:T(2,128)(2,1)} %u_hbm.1, bf16[128,128]{1,0:T(8,128)(2,1)} %og_hbm.1, bf16[3456,128]{1,0:T(8,128)(2,1)} %w_hbm.1), custom_call_target="tpu_custom_call" | custom-call | tf_op jit(solution)/shard_map/pallas_call | solution.py:297
  59.0 0.6 copy.10
  59.6 0.6 copy.11
  60.2 0.9 %copy.12 = bf16[3456,128]{1,0:T(8,128)(2,1)} copy(bf16[3456,128]{1,0:T(8,128)(2,1)S(1)} %get-tuple-element.8) | data formatting | bytes 1769472

commit v3 on v2

--- a/solution.py
+++ b/solution.py
@@ -103,42 +103,50 @@
 
     def x_copy(d, h):
         rows = pl.ds((d - 1) * 32 + h * HALF, HALF)
-        return copy(psend.at[rows], xrecv.at[rows], x_send.at[d - 1, h], x_recv.at[d - 1, h], at(d, 0))
+        return copy(psend.at[rows], xrecv.at[rows], x_send.at[h], x_recv.at[h], at(d, 0))
 
     def b_copy(h, k):
         rows = pl.ds(slot(0, h, k), 4 * ROWS)
-        return copy(zsend.at[rows], brecv.at[rows], b_send.at[h, k], b_recv.at[h, k], beside(k))
+        return copy(zsend.at[rows], brecv.at[rows], b_send.at[h], b_recv.at[h], beside(k))
 
     def a_copy(h, j):
         src = asend.at[pl.ds((h * 4 + j) * ROWS, ROWS)]
         dst = arecv.at[pl.ds(pl.multiple_of(group * ROWS, ROWS), ROWS)]
         target = {"fout": x * NZ + 16 * h + 4 * j + cls}
-        return copy(src, dst, a_send.at[h * 4 + j], a_recv.at[group], target)
+        return copy(src, dst, a_send.at[0], a_recv.at[0], target)
 
     def ga_copy(j):
         rows = pl.ds(mine, ROWS)
         target = {"fout": x * NZ + 4 * j + cls}
-        return copy(held.at[rows], held.at[rows], ga_send.at[j], ga_recv.at[group], target)
+        return copy(held.at[rows], held.at[rows], ga_send.at[0], ga_recv.at[group], target)
 
     def ga_wait(j):
         rows = pl.ds(slot(0, j // 4, 0, j % 4), ROWS)
-        return copy(held.at[rows], held.at[rows], ga_send.at[j], ga_recv.at[j], at(0, 1))
+        return copy(held.at[rows], held.at[rows], ga_send.at[0], ga_recv.at[j], at(1, 0))
 
     def gb_copy(h, k):
         src, dst = pl.ds(slot(0, h, 0), 4 * ROWS), pl.ds(slot(0, h, k), 4 * ROWS)
-        return copy(held.at[src], held.at[dst], gb_send.at[h, k], gb_recv.at[h, k], beside(4 - k))
-
-    def gx_copy(b, h, k):
-        src, dst = pl.ds(slot(0, h, k), 4 * ROWS), pl.ds(slot(b, h, k), 4 * ROWS)
-        return copy(held.at[src], held.at[dst], gx_send.at[b, h, k], gx_recv.at[b, h, k], at(-b, 0))
+        return copy(held.at[src], held.at[dst], gb_send.at[h], gb_recv.at[h], beside(4 - k))
+
+    def gx_copy(b, h, others):
+        first, rows = (1, 12 * ROWS) if others else (0, 4 * ROWS)
+        src, dst = pl.ds(slot(0, h, first), rows), pl.ds(slot(b, h, first), rows)
+        return copy(held.at[src], held.at[dst], gx_send.at[0], gx_recv.at[h, others], at(-b, 0))
+
+    def arrived(ref, rows, sem):
+        whole = ref.at[pl.ds(0, rows)]
+        copy(whole, whole, sem, sem, at(1, 0)).wait_recv()
+
+    def left(ref, rows, sem):
+        whole = ref.at[pl.ds(0, rows)]
+        copy(whole, whole, sem, sem, at(1, 0)).wait_send()
 
     def unpack(b, h, k):
         rows = pl.ds(slot(b, h, k), 4 * ROWS)
         held32[rows, :] = held[rows, :].astype(F32)
 
     def sum_x(h):
-        for d in (1, 3, 2):
-            x_copy(d, h).wait_recv()
+        arrived(xrecv, 3 * HALF, x_recv.at[h])
         for c in range(CHUNKS):
             cols = slice(c * LANES, (c + 1) * LANES)
             total = part[h * HALF : (h + 1) * HALF, cols]
@@ -152,8 +160,7 @@
             b_copy(h, k).start()
 
     def sum_b(h):
-        for k in (1, 3, 2):
-            b_copy(h, k).wait_recv()
+        arrived(brecv, 12 * ROWS, b_recv.at[h])
         total = spread[pl.ds(slot(0, h, 0), 4 * ROWS), :]
         for k in (1, 2, 3):
             total += brecv[pl.ds(slot(0, h, k), 4 * ROWS), :].astype(F32)
@@ -167,13 +174,16 @@
             def _():
                 arecv[pl.ds((h * 4 + j) * ROWS, ROWS), :] = asend[pl.ds((h * 4 + j) * ROWS, ROWS), :]
 
-    def above(h):
-        for j in range(4 * h, 4 * h + 4):
-            @pl.when(group < j)
-            def _():
-                ga_wait(j).wait_recv()
-                ga_copy(j).start()
-                a_copy(h, j - 4 * h).start()
+    def answer_row(j):
+        @pl.when(group < j)
+        def _():
+            ga_wait(j).wait_recv()
+            ga_copy(j).start()
+
+    def answer_sum(j):
+        @pl.when(group < j)
+        def _():
+            a_copy(j // 4, j % 4).start()
 
     def below(h):
         for j in range(4 * h, 4 * h + 4):
@@ -181,26 +191,20 @@
             def _():
                 ga_wait(j).wait_recv()
 
-    def gather_a(h):
+    def gather(h):
         for k in (2, 1, 3):
             gb_copy(h, k).start()
         for b in (2, 1, 3):
             gx_copy(b, h, 0).start()
         unpack(0, h, 0)
-
-    def gather_b(h):
-        for k in (1, 3, 2):
-            gb_copy(h, k).wait_recv()
-            for b in (2, 1, 3):
-                gx_copy(b, h, k).start()
+        arrived(held, 12 * ROWS, gb_recv.at[h])
+        for b in (2, 1, 3):
+            gx_copy(b, h, 1).start()
+        for k in (1, 2, 3):
             unpack(0, h, k)
 
     def finish_sums():
-        for j in range(8):
-            @pl.when(group != j)
-            def _():
-                rows = pl.ds(j * ROWS, ROWS)
-                copy(asend.at[rows], arecv.at[rows], a_send.at[j], a_recv.at[j], at(0, 1)).wait_recv()
+        arrived(arecv, 7 * ROWS, a_recv.at[0])
         upstream = arecv[0:ROWS, :].astype(F32)
         for j in range(1, 8):
             upstream += arecv[j * ROWS : (j + 1) * ROWS, :].astype(F32)
@@ -219,40 +223,59 @@
             ga_copy(j).start()
     for d in (2, 1, 3):
         x_copy(d, 0).start()
-    for d in (2, 1, 3):
-        x_copy(d, 0).wait_send()
+    left(psend, 3 * HALF, x_send.at[0])
     for d in (2, 1, 3):
         x_copy(d, 1).start()
-    for h in (0, 1):
-        sum_x(h)
-        sum_b(h)
+    sum_x(0)
+    sum_b(0)
+
+    @pl.when(group == 3)
+    def _():
+        answer_row(4)
+        answer_row(5)
+
+    sum_x(1)
+
+    @pl.when(group == 3)
+    def _():
+        answer_row(6)
+
+    sum_b(1)
 
     @pl.when(group < 3)
     def _():
-        above(0)
+        for j in (1, 2, 3):
+            answer_row(j)
+            answer_sum(j)
         below(0)
-        gather_a(0)
-        gather_b(0)
-        above(1)
-        gather_a(1)
-        gather_b(1)
+        gather(0)
+        for j in (4, 5, 6, 7):
+            answer_row(j)
+            answer_sum(j)
+        gather(1)
 
     @pl.when(group >= 3)
     def _():
-        above(1)
+        for j in (4, 5, 6):
+            @pl.when(group != 3)
+            def _():
+                answer_row(j)
+
+            answer_sum(j)
+        answer_row(7)
+        answer_sum(7)
         below(1)
-        gather_a(1)
-        gather_b(1)
+        gather(1)
         below(0)
-        gather_a(0)
-        gather_b(0)
+        gather(0)
 
     finish_sums()
-    for b in (1, 3, 2):
-        for h in (0, 1):
-            for k in range(4):
-                gx_copy(b, h, k).wait_recv()
-                unpack(b, h, k)
+    for h in (0, 1):
+        for others in (0, 1):
+            arrived(held, (36 if others else 12) * ROWS, gx_recv.at[h, others])
+            for b in (1, 2, 3):
+                for k in (1, 2, 3) if others else (0,):
+                    unpack(b, h, k)
 
     for c in range(CHUNKS):
         hidden = held32[pl.ds(c, TOK, stride=ROWS), :].astype(BF16)
@@ -261,24 +284,13 @@
         )
         dg_ref[c * LANES : (c + 1) * LANES, :] = grad.astype(BF16)
 
+    left(psend, 3 * HALF, x_send.at[1])
     for h in (0, 1):
-        if h == 1:
-            for d in (1, 2, 3):
-                x_copy(d, h).wait_send()
-        for k in (1, 2, 3):
-            b_copy(h, k).wait_send()
-            gb_copy(h, k).wait_send()
-        for j in range(4):
-            @pl.when(group != h * 4 + j)
-            def _():
-                a_copy(h, j).wait_send()
-        for b in (1, 2, 3):
-            for k in range(4):
-                gx_copy(b, h, k).wait_send()
-    for j in range(GROUPS):
-        @pl.when(group != j)
-        def _():
-            ga_copy(j).wait_send()
+        left(zsend, 12 * ROWS, b_send.at[h])
+        left(held, 12 * ROWS, gb_send.at[h])
+    left(asend, 7 * ROWS, a_send.at[0])
+    left(held, 7 * ROWS, ga_send.at[0])
+    left(held, 96 * ROWS, gx_send.at[0])
 
 
 def local(gate_pre, up_pre, out_grad, down_weight):
@@ -319,12 +331,12 @@
             pltpu.VMEM((TOK * ROWS, LANES), BF16),
             pltpu.VMEM((TOK * ROWS, LANES), F32),
             dma((4,)),
-            dma((3, 2)), dma((3, 2)),
-            dma((2, 4)), dma((2, 4)),
-            dma((8,)), dma((8,)),
-            dma((8,)), dma((8,)),
-            dma((2, 4)), dma((2, 4)),
-            dma((4, 2, 4)), dma((4, 2, 4)),
+            dma((2,)), dma((2,)),
+            dma((2,)), dma((2,)),
+            dma((1,)), dma((1,)),
+            dma((1,)), dma((8,)),
+            dma((2,)), dma((2,)),
+            dma((1,)), dma((2, 2)),
         ],
         compiler_params=pltpu.CompilerParams(
             collective_id=0, has_side_effects=True, vmem_limit_bytes=32 * 2**20

time: 61.3 us -> 59 us (0.962)
  the two profiles are of different devices: /device:TPU:992 before, /device:TPU:920 now
where the time goes in v3:
time: 59 us; the launch traced here: 58.8 us
  Pallas kernels  56.1 us (95%)
  local copies, waits for them, and re-layouts  2.11 us (4%)
  between operations  0.64 us (1%)
    pallas_call x1, Pallas kernels, local(): pl.pallas_call(kernel, out_shape=shapes, in_specs=[anywhere] * 4, out_spe...  56.1 us
    unnamed x3, local copies, waits for them, and re-layouts  2.11 us

profile of v3, /device:TPU:920, one launch (start us, length us, event | category | flops | bytes accessed | tf_op | source)
XLA Modules:
  0.0 58.8 jit_solution(16285186790923702181)
XLA Ops:
  0.6 56.1 %shard_map.67 = (bf16[1,3456]{1,0:T(2,128)(2,1)S(1)}, bf16[1,3456]{1,0:T(2,128)(2,1)S(1)}, bf16[3456,128]{1,0:T(8,128)(2,1)S(1)}) custom-call(bf16[1,3456]{1,0:T(2,128)(2,1)} %g_hbm.1, bf16[1,3456]{1,0:T(2,128)(2,1)} %u_hbm.1, bf16[128,128]{1,0:T(8,128)(2,1)} %og_hbm.1, bf16[3456,128]{1,0:T(8,128)(2,1)} %w_hbm.1), custom_call_target="tpu_custom_call" | custom-call | tf_op jit(solution)/shard_map/pallas_call | solution.py:309
  56.7 0.6 %copy.10 = bf16[1,3456]{1,0:T(2,128)(2,1)} copy(bf16[1,3456]{1,0:T(2,128)(2,1)S(1)} %get-tuple-element.6) | data formatting | bytes 13824
  57.3 0.6 %copy.11 = bf16[1,3456]{1,0:T(2,128)(2,1)} copy(bf16[1,3456]{1,0:T(2,128)(2,1)S(1)} %get-tuple-element.7) | data formatting | bytes 13824
  57.9 0.9 %copy.12 = bf16[3456,128]{1,0:T(8,128)(2,1)} copy(bf16[3456,128]{1,0:T(8,128)(2,1)S(1)} %get-tuple-element.8) | data formatting | bytes 1769472

commit v4 on v3

--- a/solution.py
+++ b/solution.py
@@ -185,18 +185,24 @@
         def _():
             a_copy(j // 4, j % 4).start()
 
-    def below(h):
-        for j in range(4 * h, 4 * h + 4):
+    def below(h, end=4, start=0):
+        for j in range(4 * h + start, 4 * h + end):
             @pl.when(group > j)
             def _():
                 ga_wait(j).wait_recv()
 
     def gather(h):
+        gather_start(h)
+        gather_end(h)
+
+    def gather_start(h):
         for k in (2, 1, 3):
             gb_copy(h, k).start()
         for b in (2, 1, 3):
             gx_copy(b, h, 0).start()
         unpack(0, h, 0)
+
+    def gather_end(h):
         arrived(held, 12 * ROWS, gb_recv.at[h])
         for b in (2, 1, 3):
             gx_copy(b, h, 1).start()
@@ -234,9 +240,13 @@
         answer_row(4)
         answer_row(5)
 
+    @pl.when(group >= 4)
+    def _():
+        answer_row(5)
+
     sum_x(1)
 
-    @pl.when(group == 3)
+    @pl.when(group >= 3)
     def _():
         answer_row(6)
 
@@ -249,25 +259,25 @@
             answer_sum(j)
         below(0)
         gather(0)
-        for j in (4, 5, 6, 7):
+        for j in (5, 6, 7, 4):
             answer_row(j)
+        gather_start(1)
+        for j in (7, 6, 5, 4):
             answer_sum(j)
-        gather(1)
+        gather_end(1)
 
     @pl.when(group >= 3)
     def _():
-        for j in (4, 5, 6):
-            @pl.when(group != 3)
-            def _():
-                answer_row(j)
-
+        answer_row(7)
+        for j in (7, 6, 5, 4):
             answer_sum(j)
-        answer_row(7)
-        answer_sum(7)
         below(1)
-        gather(1)
-        below(0)
-        gather(0)
+        gather_start(1)
+        below(0, 2)
+        gather_end(1)
+        below(0, 4, 2)
+        gather_start(0)
+        gather_end(0)
 
     finish_sums()
     for h in (0, 1):

time: 59 us -> 56.8 us (0.963)
  the two profiles are of different devices: /device:TPU:920 before, /device:TPU:768 now
where the time goes in v4:
time: 56.8 us; the launch traced here: 56.6 us
  Pallas kernels  53.9 us (95%)
  local copies, waits for them, and re-layouts  2.11 us (4%)
  between operations  0.64 us (1%)
    pallas_call x1, Pallas kernels, local(): pl.pallas_call(kernel, out_shape=shapes, in_specs=[anywhere] * 4, out_spe...  53.9 us
    unnamed x3, local copies, waits for them, and re-layouts  2.11 us

profile of v4, /device:TPU:768, one launch (start us, length us, event | category | flops | bytes accessed | tf_op | source)
XLA Modules:
  0.0 56.6 jit_solution(9234224780993821718)
XLA Ops:
  0.6 53.9 %shard_map.67 = (bf16[1,3456]{1,0:T(2,128)(2,1)S(1)}, bf16[1,3456]{1,0:T(2,128)(2,1)S(1)}, bf16[3456,128]{1,0:T(8,128)(2,1)S(1)}) custom-call(bf16[1,3456]{1,0:T(2,128)(2,1)} %g_hbm.1, bf16[1,3456]{1,0:T(2,128)(2,1)} %u_hbm.1, bf16[128,128]{1,0:T(8,128)(2,1)} %og_hbm.1, bf16[3456,128]{1,0:T(8,128)(2,1)} %w_hbm.1), custom_call_target="tpu_custom_call" | custom-call | tf_op jit(solution)/shard_map/pallas_call | solution.py:319
  54.5 0.6 %copy.10 = bf16[1,3456]{1,0:T(2,128)(2,1)} copy(bf16[1,3456]{1,0:T(2,128)(2,1)S(1)} %get-tuple-element.6) | data formatting | bytes 13824
  55.1 0.6 %copy.11 = bf16[1,3456]{1,0:T(2,128)(2,1)} copy(bf16[1,3456]{1,0:T(2,128)(2,1)S(1)} %get-tuple-element.7) | data formatting | bytes 13824
  55.7 0.9 %copy.12 = bf16[3456,128]{1,0:T(8,128)(2,1)} copy(bf16[3456,128]{1,0:T(8,128)(2,1)S(1)} %get-tuple-element.8) | data formatting | bytes 1769472

commit v5 on v4

--- a/solution.py
+++ b/solution.py
@@ -330,7 +330,7 @@
             pltpu.VMEM((32, UNITS), F32),
             pltpu.VMEM((96, UNITS), BF16),
             pltpu.VMEM((96, UNITS), BF16),
-            pltpu.VMEM((32 * ROWS, LANES), F32),
+            pltpu.VMEM((33 * ROWS, LANES), F32),
             pltpu.VMEM((32 * ROWS, LANES), BF16),
             pltpu.VMEM((32 * ROWS, LANES), BF16),
             pltpu.VMEM((8 * ROWS, LANES), BF16),
@@ -339,7 +339,7 @@
             pltpu.VMEM((ROWS, LANES), F32),
             pltpu.VMEM((2 * ROWS, LANES), F32),
             pltpu.VMEM((TOK * ROWS, LANES), BF16),
-            pltpu.VMEM((TOK * ROWS, LANES), F32),
+            pltpu.VMEM((TOK * ROWS + ROWS, LANES), F32),
             dma((4,)),
             dma((2,)), dma((2,)),
             dma((2,)), dma((2,)),

time: 56.8 us -> 56.8 us (level)
  no operation moved by 1% of the time
where the time goes in v5:
time: 56.8 us; the launch traced here: 56.6 us
  Pallas kernels  53.9 us (95%)
  local copies, waits for them, and re-layouts  2.11 us (4%)
  between operations  0.64 us (1%)
    pallas_call x1, Pallas kernels, local(): pl.pallas_call(kernel, out_shape=shapes, in_specs=[anywhere] * 4, out_spe...  53.9 us
    unnamed x3, local copies, waits for them, and re-layouts  2.11 us

profile of v5, /device:TPU:768, one launch (start us, length us, event | category | flops | bytes accessed | tf_op | source)
XLA Modules:
  0.0 56.6 jit_solution(17453615086262449208)
XLA Ops:
  0.6 53.9 %shard_map.67 = (bf16[1,3456]{1,0:T(2,128)(2,1)S(1)}, bf16[1,3456]{1,0:T(2,128)(2,1)S(1)}, bf16[3456,128]{1,0:T(8,128)(2,1)S(1)}) custom-call(bf16[1,3456]{1,0:T(2,128)(2,1)} %g_hbm.1, bf16[1,3456]{1,0:T(2,128)(2,1)} %u_hbm.1, bf16[128,128]{1,0:T(8,128)(2,1)} %og_hbm.1, bf16[3456,128]{1,0:T(8,128)(2,1)} %w_hbm.1), custom_call_target="tpu_custom_call" | custom-call | tf_op jit(solution)/shard_map/pallas_call | solution.py:319
  54.5 0.6 %copy.10 = bf16[1,3456]{1,0:T(2,128)(2,1)} copy(bf16[1,3456]{1,0:T(2,128)(2,1)S(1)} %get-tuple-element.6) | data formatting | bytes 13824
  55.1 0.6 %copy.11 = bf16[1,3456]{1,0:T(2,128)(2,1)} copy(bf16[1,3456]{1,0:T(2,128)(2,1)S(1)} %get-tuple-element.7) | data formatting | bytes 13824
  55.7 0.9 %copy.12 = bf16[3456,128]{1,0:T(8,128)(2,1)} copy(bf16[3456,128]{1,0:T(8,128)(2,1)S(1)} %get-tuple-element.8) | data formatting | bytes 1769472
